TPU v7x, 32 devices: a whole 2x2x4 slice. The times are simulated.
32 devices in a mesh: seq: 8 (over z, y), tensor: 4 (over x, core).
Axes of the slice: x: 2, y: 2, z: 4, core: 2. Of those that a mesh axis runs over, the one named last changes fastest.
Arguments:
- tokens: bfloat16 [128, 4, 3072], P('seq'), may hold values from -6 to 6
- lengths: int32 [128], replicated, may hold values from 1 to 16384, as said below
- page_request: int32 [1024], P('seq'), may hold values from 0 to 127, as said below
- page_block: int32 [1024], P('seq'), may hold values from 0 to 128, as said below
- k_cache: bfloat16 [1024, 8, 128, 128], P('seq', 'tensor'), may hold values from -330 to 330
- v_cache: bfloat16 [1024, 8, 128, 128], P('seq', 'tensor'), may hold values from -6 to 6
- attn_gain: bfloat16 [3072], replicated, may hold values from 0.099609375 to 1.8984375
- w_query: bfloat16 [3072, 3072], P(None, 'tensor'), may hold values from -0.109375 to 0.109375
- w_key: bfloat16 [3072, 1024], P(None, 'tensor'), may hold values from -0.109375 to 0.109375
- w_value: bfloat16 [3072, 1024], P(None, 'tensor'), may hold values from -0.109375 to 0.109375
- w_out: bfloat16 [3072, 3072], P('tensor'), may hold values from -0.109375 to 0.109375
- mlp_gain: bfloat16 [3072], replicated, may hold values from 0.099609375 to 1.8984375
- w_gate: bfloat16 [3072, 4096], P(None, 'tensor'), may hold values from -0.109375 to 0.109375
- w_up: bfloat16 [3072, 4096], P(None, 'tensor'), may hold values from -0.109375 to 0.109375
- w_down: bfloat16 [4096, 3072], P('tensor'), may hold values from -0.09375 to 0.09375
Outputs:
- layer_out: bfloat16 [128, 4, 3072], P('seq', None, 'tensor')
Inputs may be any that keep to these rules, and one draw needn't show every extreme that they name: `lengths`: A request r whose index is a multiple of 32 has a long cache, within 128 tokens of 16384; the others have at most 511. Request 0 has exactly 16384. `page_request`: each pair of a long request and a page number below 128, or of a short request and a page number below 4, appears in exactly one slot; slots of pages at or beyond a request's length hold no used position. A short request's pages lie in the slots of the seq index that holds its tokens. `page_block`: slots of page number 128 hold no used position.
All inputs are finite; a program needn't handle non-finite values.
Results may differ from a plain program's by a relative error of at most 0.012.
Values may be sent and summed in bfloat16 or wider, within the bound.
A program may use at most 128 MiB of HBM per device.

v0:
```python
import math

import jax
import jax.numpy as jnp
from jax import lax
from jax.sharding import PartitionSpec as P

EPSILON = 1e-05
NEGATIVE = -1e30
ROPE_BASE = 500000.0


def rms_norm(values, gains):
    mean_square = jnp.mean(values * values, axis=-1, keepdims=True)
    return values * lax.rsqrt(mean_square + EPSILON) * gains.astype(jnp.float32)


def rotary(values, position):
    head_width = values.shape[-1]
    half_width = head_width // 2
    inverse = 1.0 / ROPE_BASE ** (jnp.arange(half_width, dtype=jnp.float32) * 2.0 / head_width)
    angle = position.astype(jnp.float32)[..., None, None] * inverse
    cosine = jnp.cos(angle)
    sine_table = jnp.sin(angle)
    front_half = values[..., :half_width]
    back_half = values[..., half_width:]
    return jnp.concatenate(
        [
            front_half * cosine - back_half * sine_table,
            back_half * cosine + front_half * sine_table,
        ],
        axis=-1,
    )


def per_device(
    tokens,
    lengths,
    page_request,
    page_block,
    k_cache,
    v_cache,
    attn_gain,
    w_query,
    w_key,
    w_value,
    w_out,
    mlp_gain,
    w_gate,
    w_up,
    w_down,
):
    req_dev, fresh_count, model_width = tokens.shape
    head_dim = k_cache.shape[-1]
    page_len = k_cache.shape[2]
    kv_local = k_cache.shape[1]
    group_size = w_query.shape[1] // (kv_local * head_dim)
    lanes = fresh_count * group_size
    row_count = req_dev * fresh_count
    score_scale = 1.0 / math.sqrt(head_dim)
    seq_index = lax.axis_index("seq")
    home_row = seq_index * req_dev
    own_length = lax.dynamic_slice_in_dim(lengths, home_row, req_dev)
    position = own_length[:, None] + jnp.arange(fresh_count, dtype=jnp.int32)[None, :]
    values_in = tokens.astype(jnp.float32)
    normed_in = rms_norm(values_in, attn_gain).astype(jnp.bfloat16).reshape(row_count, model_width)
    queries = jnp.dot(normed_in, w_query, preferred_element_type=jnp.float32).reshape(
        req_dev, fresh_count, kv_local * group_size, head_dim
    )
    queries = rotary(queries, position).astype(jnp.bfloat16)
    queries = queries.reshape(req_dev, fresh_count, kv_local, group_size, head_dim).transpose(
        0, 2, 1, 3, 4
    )
    queries = queries.reshape(req_dev, kv_local, lanes, head_dim)
    key_new = jnp.dot(normed_in, w_key, preferred_element_type=jnp.float32).reshape(
        req_dev, fresh_count, kv_local, head_dim
    )
    key_new = rotary(key_new, position).astype(jnp.bfloat16).transpose(0, 2, 1, 3)
    value_new = jnp.dot(normed_in, w_value, preferred_element_type=jnp.float32).astype(jnp.bfloat16)
    value_new = value_new.reshape(req_dev, fresh_count, kv_local, head_dim).transpose(0, 2, 1, 3)
    requests = lengths.shape[0]
    owner_member = page_request[:, None] == jnp.arange(requests, dtype=jnp.int32)[None, :]
    owner_length = jnp.sum(jnp.where(owner_member, lengths[None, :], 0), axis=1)
    offsets = jnp.arange(page_len, dtype=jnp.int32)
    is_valid = page_block[:, None] * page_len + offsets[None, :] < owner_length[:, None]
    fresh_scores = (
        jnp.einsum("rhqd,rhsd->rhqs", queries, key_new, preferred_element_type=jnp.float32)
        * score_scale
    )
    causal = (jnp.arange(lanes, dtype=jnp.int32) // group_size)[:, None] >= jnp.arange(
        fresh_count, dtype=jnp.int32
    )[None, :]
    fresh_scores = jnp.where(causal[None, None], fresh_scores, NEGATIVE)
    fresh_top = jnp.max(fresh_scores, axis=-1)
    every_query = lax.all_gather(
        queries.reshape(req_dev, kv_local * lanes * head_dim), "seq", axis=0, tiled=True
    )
    chosen = every_query[page_request].reshape(-1, kv_local, lanes, head_dim)
    scores = (
        jnp.einsum("phqd,phkd->phqk", chosen, k_cache, preferred_element_type=jnp.float32)
        * score_scale
    )
    scores = jnp.where(is_valid[:, None, None, :], scores, NEGATIVE)
    page_max = jnp.max(scores, axis=-1)
    cache_max = jnp.max(
        jnp.where(owner_member[:, :, None, None], page_max[:, None], NEGATIVE), axis=0
    )
    own_max = jnp.maximum(lax.dynamic_slice_in_dim(cache_max, home_row, req_dev, 0), fresh_top)
    candidate = lax.dynamic_update_slice_in_dim(cache_max, own_max, home_row, 0)
    row_max = lax.pmax(candidate, "seq")
    page_ref = jnp.sum(jnp.where(owner_member[:, :, None, None], row_max[None], 0.0), axis=1)
    weights = jnp.where(
        is_valid[:, None, None, :], jnp.exp(scores - page_ref[..., None]), 0.0
    ).astype(jnp.bfloat16)
    page_total = jnp.sum(weights.astype(jnp.float32), axis=-1)
    page_sum = jnp.einsum("phqk,phkd->phqd", weights, v_cache, preferred_element_type=jnp.float32)
    member_float = owner_member.astype(jnp.float32)
    slot_total = jnp.einsum(
        "pr,phq->rhq", member_float, page_total, precision=lax.Precision.HIGHEST
    )
    slot_summed = jnp.einsum(
        "pr,phqd->rhqd", member_float, page_sum, precision=lax.Precision.HIGHEST
    )
    total_all, summed_all = lax.psum((slot_total, slot_summed), "seq")
    own_total = lax.dynamic_slice_in_dim(total_all, home_row, req_dev, 0)
    own_summed = lax.dynamic_slice_in_dim(summed_all, home_row, req_dev, 0)
    own_ref = lax.dynamic_slice_in_dim(row_max, home_row, req_dev, 0)
    fresh_weights = jnp.where(
        causal[None, None], jnp.exp(fresh_scores - own_ref[..., None]), 0.0
    ).astype(jnp.bfloat16)
    own_total = own_total + jnp.sum(fresh_weights.astype(jnp.float32), axis=-1)
    own_summed = own_summed + jnp.einsum(
        "rhqs,rhsd->rhqd", fresh_weights, value_new, preferred_element_type=jnp.float32
    )
    attended = (own_summed / own_total[..., None]).astype(jnp.bfloat16)
    attended = attended.reshape(req_dev, kv_local, fresh_count, group_size, head_dim).transpose(
        0, 2, 1, 3, 4
    )
    attended = attended.reshape(row_count, kv_local * group_size * head_dim)
    partial_value = jnp.dot(attended, w_out, preferred_element_type=jnp.float32)
    flat_input = values_in.reshape(row_count, model_width)
    col_count = model_width // lax.axis_size("tensor")
    col_start = lax.axis_index("tensor") * col_count
    attn_sum = lax.psum(partial_value, "tensor")
    residual = (flat_input + attn_sum).astype(jnp.bfloat16)
    normed = rms_norm(residual.astype(jnp.float32), mlp_gain).astype(jnp.bfloat16)
    own_residual = lax.dynamic_slice_in_dim(residual, col_start, col_count, 1)
    gate_out = jnp.dot(normed, w_gate, preferred_element_type=jnp.float32)
    up_out = jnp.dot(normed, w_up, preferred_element_type=jnp.float32)
    activated = (jax.nn.silu(gate_out) * up_out).astype(jnp.bfloat16)
    down_out = jnp.dot(activated, w_down, preferred_element_type=jnp.float32)
    mlp_part = lax.psum_scatter(down_out, "tensor", scatter_dimension=1, tiled=True)
    layer_out = (own_residual.astype(jnp.float32) + mlp_part).astype(jnp.bfloat16)
    return layer_out.reshape(req_dev, fresh_count, col_count)


def solution(mesh):
    placed = (
        P("seq", None, None),
        P(),
        P("seq"),
        P("seq"),
        P("seq", "tensor", None, None),
        P("seq", "tensor", None, None),
        P(),
        P(None, "tensor"),
        P(None, "tensor"),
        P(None, "tensor"),
        P("tensor", None),
        P(),
        P(None, "tensor"),
        P(None, "tensor"),
        P("tensor", None),
    )
    return jax.shard_map(
        per_device, mesh=mesh, in_specs=placed, out_specs=P("seq", None, "tensor"), check_vma=False
    )
```

profile of v0, /device:TPU:0, one launch (start us, length us, event | category | flops | bytes accessed | tf_op | source)
XLA Modules:
  0.0 296.6 jit_solution(696603345898927171)
XLA Ops:
  6.6 0.8 dynamic_slice.18
  7.4 1.3 multiply_reduce_fusion
  9.4 6.7 %copy.83 = bf16[3072,768]{0,1:T(8,128)(2,1)} copy(bf16[3072,768]{1,0:T(8,128)(2,1)} %param.22) | data formatting | bytes 9437184 | tf_op args[7]
  16.6 3.9 %fusion.11 = f32[16,4,6,128]{3,0,2,1:T(8,128)S(1)} fusion(bf16[6,128,3072,1]{2,1,0,3:T(8,128)(2,1)} %bitcast.49, bf16[16,4,3072,1]{2,1,0,3:T(4,128)(2,1)S(1)} %fusion.53), kind=kOutput, calls=%fused_computation.25 | convolution fusion | flops 301989888 | bytes 5308416 | tf_op jit(solution)/shard_map/dot_general | solution.py:67
  22.1 2.6 copy.115
  24.7 2.0 fusion.9
  28.6 33.8 %all_gather.3 = bf16[128,3072]{1,0:T(8,128)(2,1)S(1)} all-gather(bf16[16,3072]{1,0:T(8,128)(2,1)S(1)} %reshape_reshape.3), channel_id=1, replica_groups=mesh['seq'=8,'tensor'=4] {'seq'}, dimensions={0}, use_global_device_ids=true | all-gather | bytes 884736 | tf_op jit(solution)/shard_map/all_gather | solution.py:95
  62.4 1.0 gather_fusion
  63.8 1.7 copy.89
  66.3 9.6 %fusion = (f32[128,2,12]{2,1,0:T(2,128)S(1)}, f32[128,2,12,128]{3,2,1,0:T(8,128)}) fusion(pred[128,128]{1,0:T(8,128)(4,1)S(1)} %add_compare_fusion, bf16[128,2,12,128]{3,2,1,0:T(8,128)(2,1)} %copy.89, bf16[128,2,128,128]{3,2,1,0:T(8,128)(2,1)} %param.19), kind=kOutput, calls=%fused_computation.4 | convolution fusion | flops 101839872 | bytes 10776576 | tf_op jit(solution)/shard_map/phqd,phkd->phqk/dot_general | solution.py:100
  76.9 37.4 %pmax.7 = f32[128,2,12]{0,2,1:T(8,128)S(1)} all-reduce(f32[128,2,12]{0,2,1:T(8,128)S(1)} %dynamic_update_slice.3), channel_id=1, replica_groups=mesh['seq'=8,'tensor'=4] {'seq'}, use_global_device_ids=true, to_apply=%region_5.6 | all-reduce | flops 3072 | bytes 24576 | tf_op jit(solution)/shard_map/pmax | solution.py:110
  114.9 6.4 %fusion.37 = f32[128,2,12,128]{3,2,1,0:T(8,128)S(1)} fusion(bf16[128,2,128,128]{3,2,1,0:T(8,128)(2,1)} %param.20, f32[128,2,12,128]{3,2,1,0:T(8,128)} %get-tuple-element.14, f32[128,2,12]{2,1,0:T(2,128)S(1)} %copy.97, pred[128,128]{1,0:T(8,128)(4,1)S(1)} %add_compare_fusion), kind=kOutput, calls=%fused_computation.79 | convolution fusion | flops 102629376 | bytes 11563008 | tf_op jit(solution)/shard_map/phqk,phkd->phqd/dot_general | solution.py:116
  121.3 3.0 %fusion.1 = f32[128,2,12,128]{3,0,2,1:T(8,128)} fusion(f32[128,2,12,128]{3,2,1,0:T(8,128)S(1)} %fusion.37, s32[128]{0:T(128)S(1)} %copy-done.9), kind=kOutput, calls=%fused_computation.5 | convolution fusion | flops 603996160 | bytes 3146240 | tf_op jit(solution)/shard_map/pr,phqd->rhqd/dot_general | solution.py:121
  124.4 2.6 convert_reduce_fusion
  127.4 35.9 %psum.22 = f32[128,2,12]{2,0,1:T(8,128)S(1)} all-reduce(f32[128,2,12]{2,0,1:T(8,128)S(1)} %fusion.20), channel_id=1, replica_groups=mesh['seq'=8,'tensor'=4] {'seq'}, use_global_device_ids=true, to_apply=%region_9.10 | all-reduce | flops 3072 | bytes 24576 | tf_op jit(solution)/shard_map/psum | solution.py:124
  164.5 47.6 %all-reduce.3.cloned.1.call-done = f32[128,2,12,128]{3,0,2,1:T(8,128)} async-done(((f32[128,2,12,128]{3,0,2,1:T(8,128)}), f32[128,2,12,128]{3,0,2,1:T(8,128)}) %all-reduce.3.cloned.1.call-update) | async-done | bytes 1572880 | tf_op jit(solution)/shard_map/psum | solution.py:124
  212.2 1.1 fusion.19
  213.4 4.2 %fusion.39 = f32[64,3072]{1,0:T(8,128)} fusion(bf16[64,768]{1,0:T(8,128)(2,1)S(1)} %reshape.187, bf16[768,3072]{1,0:T(8,128)(2,1)} %param.25), kind=kOutput, calls=%fused_computation.81 | convolution fusion | flops 301989888 | bytes 5603328 | tf_op jit(solution)/shard_map/dot_general | solution.py:140
  217.7 34.0 %all-reduce.5.cloned.1.call-done = f32[64,3072]{1,0:T(8,128)} async-done(((f32[64,3072]{1,0:T(8,128)}), f32[64,3072]{1,0:T(8,128)}) %all-reduce.5.cloned.1.call-update) | async-done | bytes 786448 | tf_op jit(solution)/shard_map/psum | solution.py:144
  251.7 1.3 fusion.6
  253.1 4.0 %fusion.26 = f32[64,1024]{1,0:T(8,128)S(1)} fusion(bf16[3072,1024]{1,0:T(8,128)(2,1)} %param.27, bf16[64,3072]{1,0:T(8,128)(2,1)S(1)} %get-tuple-element.6, f32[3072]{0:T(1024)S(1)} %convert_element_type.73, f32[64]{0:T(128)S(1)} %add_rsqrt_fusion.1), kind=kOutput, calls=%fused_computation.43 | convolution fusion | flops 403439616 | bytes 6959360 | tf_op jit(solution)/shard_map/dot_general | solution.py:148
  257.1 7.8 %fusion.5 = f32[64,3072]{1,0:T(8,128)} fusion(bf16[1024,3072]{1,0:T(8,128)(2,1)} %param.29, bf16[3072,1024]{1,0:T(8,128)(2,1)} %param.28, f32[64,1024]{1,0:T(8,128)S(1)} %fusion.26, bf16[64,3072]{1,0:T(8,128)(2,1)S(1)} %get-tuple-element.6, f32[3072]{0:T(1024)S(1)} %convert_element_type.73, f32[64]{0:T(128)S(1)} %add_rsqrt_fusion.1), kind=kOutput, calls=%fused_computation.14 | convolution fusion | flops 806486016 | bytes 14037248 | tf_op jit(solution)/shard_map/dot_general | solution.py:151
  265.0 23.4 %reduce-scatter.2.cloned.1.call-done = f32[64,768]{1,0:T(8,128)} async-done(((f32[64,3072]{1,0:T(8,128)}), f32[64,768]{1,0:T(8,128)}) %reduce-scatter.2.cloned.1.call-update) | async-done | bytes 196624 | tf_op jit(solution)/shard_map/reduce_scatter | solution.py:152
  288.5 0.9 add_convert_fusion.1
  (83 shorter events, 10.0 us)
Async XLA Ops:
  6.5 157.3 %copy-start = (bf16[3072,256]{1,0:T(8,128)(2,1)S(1)}, bf16[3072,256]{1,0:T(8,128)(2,1)}, u32[]{:S(2)}) copy-start(bf16[3072,256]{1,0:T(8,128)(2,1)} %param.24) | copy-start | bytes 4718596
  6.5 205.6 %all-reduce.3.cloned.1.call-start = ((), (), s32[]{:S(2)}) async-start(), calls=%async_computation.1 | async-start | bytes 3145728 | tf_op jit(solution)/shard_map/psum | solution.py:124
  8.7 7.6 %copy-start.3 = (f32[16,4]{1,0:T(8,128)}, f32[16,4]{1,0:T(8,128)S(1)}, u32[]{:S(2)}) copy-start(f32[16,4]{1,0:T(8,128)S(1)} %add_rsqrt_fusion) | copy-start | bytes 772
  9.4 6.9 %copy-start.1 = (bf16[16,4,3072]{2,1,0:T(4,128)(2,1)S(1)}, bf16[16,4,3072]{2,1,0:T(4,128)(2,1)}, u32[]{:S(2)}) copy-start(bf16[16,4,3072]{2,1,0:T(4,128)(2,1)} %param.15) | copy-start | bytes 1179652
  16.6 4.3 %copy-start.8 = (s32[128]{0:T(128)S(1)}, s32[128]{0:T(128)}, u32[]{:S(2)}) copy-start(s32[128]{0:T(128)} %param.17) | copy-start | bytes 1540
  16.6 4.3 %copy-start.13 = (s32[128]{0:T(128)S(1)}, s32[128]{0:T(128)}, u32[]{:S(2)}) copy-start(s32[128]{0:T(128)} %param.16) | copy-start | bytes 1540
  26.9 1.7 copy-start.10
  63.5 2.7 copy-start.12
  66.3 9.7 %copy-start.6 = (pred[128,128]{0,1:T(8,128)(4,1)S(1)}, pred[128,128]{0,1:T(8,128)(4,1)}, u32[]{:S(2)}) copy-start(pred[128,128]{0,1:T(8,128)(4,1)} %iota_compare_fusion) | copy-start | bytes 49156
  66.3 10.4 %copy-start.5 = (f32[16,2,12]{0,2,1:T(8,128)S(1)}, f32[16,2,12]{0,2,1:T(8,128)}, u32[]{:S(2)}) copy-start(f32[16,2,12]{0,2,1:T(8,128)} %copy.96) | copy-start | bytes 4612
  114.9 6.4 %copy-start.9 = (s32[128]{0:T(128)S(1)}, s32[128]{0:T(128)}, u32[]{:S(2)}) copy-start(s32[128]{0:T(128)} %param.17) | copy-start | bytes 1540
  124.3 38.9 %copy-start.2 = (f32[16,2,12,4]{2,3,1,0:T(4,128)S(1)}, f32[16,2,12,4]{2,3,1,0:T(4,128)}, u32[]{:S(2)}) copy-start(f32[16,2,12,4]{2,3,1,0:T(4,128)} %get-tuple-element.16) | copy-start | bytes 18436
  124.3 38.9 %copy-start.11 = (pred[12,4]{0,1:T(4,128)(4,1)S(1)}, pred[12,4]{0,1:T(4,128)(4,1)}, u32[]{:S(2)}) copy-start(pred[12,4]{0,1:T(4,128)(4,1)} %copy-done.10) | copy-start | bytes 148
  124.3 39.1 %copy-start.4 = (f32[16,4]{1,0:T(8,128)S(1)}, f32[16,4]{1,0:T(8,128)}, u32[]{:S(2)}) copy-start(f32[16,4]{1,0:T(8,128)} %copy-done.3) | copy-start | bytes 772
  124.4 127.4 %all-reduce.5.cloned.1.call-start = ((), (), s32[]{:S(2)}) async-start(), calls=%async_computation.2 | async-start | bytes 1572864 | tf_op jit(solution)/shard_map/psum | solution.py:144
  213.4 4.3 %copy-start.7 = (bf16[3072]{0:T(1024)(128)(2,1)S(1)}, bf16[3072]{0:T(1024)(128)(2,1)}, u32[]{:S(2)}) copy-start(bf16[3072]{0:T(1024)(128)(2,1)} %param.26) | copy-start | bytes 18436
  217.6 70.9 %reduce-scatter.2.cloned.1.call-start = ((), (), s32[]{:S(2)}) async-start(), calls=%async_computation.3 | async-start | bytes 983040 | tf_op jit(solution)/shard_map/reduce_scatter | solution.py:152
Sparse Core Ops, SparseCore 0:
  124.5 87.6 all-reduce.2
  217.7 33.9 all-reduce.4
  265.1 23.2 reduce-scatter.1
where the time goes:
time: 297 us
  blocking collectives  107 us (36%)
  waiting for transfers between devices  105 us (35%)
  matrix products  42.7 us (14%)
  local copies, waits for them, and re-layouts  15.9 us (5%)
  between operations  13.5 us (5%)
  other arithmetic  12.4 us (4%)
    psum x1, waiting for transfers between devices, per_device(): total_all, summed_all = lax.psum((slot_total, slot_summed), 'seq')  47.6 us
    pmax x1, blocking collectives, per_device(): row_max = lax.pmax(candidate, 'seq')  37.4 us
    psum x1, blocking collectives, per_device(): total_all, summed_all = lax.psum((slot_total, slot_summed), 'seq')  35.9 us
    psum x1, waiting for transfers between devices, per_device(): attn_sum = lax.psum(partial_value, 'tensor')  34 us
    all_gather x1, blocking collectives, per_device(): lax.all_gather(queries.reshape(req_dev, kv_local * lanes * head_dim), 'se...  33.8 us
    reduce_scatter x1, waiting for transfers between devices, per_device(): lax.psum_scatter(down_out, 'tensor', scatter_dimension=1, tiled=True)  23.4 us
    dot_general x1, matrix products, per_device(): jnp.einsum('phqd,phkd->phqk', chosen, k_cache, preferred_element_type=jnp...  9.63 us
    dot_general x1, matrix products, per_device(): down_out = jnp.dot(activated, w_down, preferred_element_type=jnp.float32)  7.85 us
  transfers between devices with their start and end apart: 3, of which 3 were waited for; matrix products, arithmetic and copies ran while one was open for 1% of the time, Pallas kernels for 0%

commit v1 on v0

v1 whole, which is shorter than its diff:
```python
import functools
import math

import jax
import jax.numpy as jnp
from jax import lax
from jax.experimental import pallas as pl
from jax.experimental.pallas import tpu as pltpu
from jax.sharding import PartitionSpec as P

EPSILON = 1e-05
NEGATIVE = -1e30
FLOOR = -1e20
ROPE_BASE = 500000.0
STRIDE = 32
SHORT_BLK = 4
ROWS = 16
UNROLL = 8
MESH = pl.DeviceIdType.MESH
F32 = jnp.float32
BF16 = jnp.bfloat16


def mm(a, b):
    return jnp.dot(a, b, preferred_element_type=F32)


def mm_t(a, b):
    return lax.dot_general(a, b, (((1,), (1,)), ((), ())), preferred_element_type=F32)


def layer_kernel(
    seqs, tens, n_long, others, req_dev, fresh, group, kv,
    ids, tok, gain1, gain2, cos, sin, wq, wk, wv, wo, wg, wu, wd, kc, vc,
    out,
    wq_v, wk_v, wv_v, wo_v, wg_v, wu_v, wd_v, kc_v, vc_v,
    nrm, qkv, qf, kf, vf, qs, ks, vs, so, sm, sl, ql, oo, om, ol, mj, pj, parts,
    att, s1, r1, own, s2, r2, res, act, s4, r4, s5, r5,
    w_sem, qsend, qrecv, psend, precv,
    s1_sem, r1_sem, s2_sem, r2_sem, s3_sem, r3_sem, s4_sem, r4_sem, s5_sem, r5_sem,
):
    s = lax.axis_index("seq")
    t = lax.axis_index("tensor")
    c = lax.rem(t, 2)
    x = t // 2
    xs = tens // 2
    step = STRIDE // req_dev
    rows, width = tok.shape
    bw = width // tens
    head = kc.shape[-1]
    page = kc.shape[2]
    scale = 1.0 / math.sqrt(head)
    mate = (s, t + 1 - 2 * c)
    lane_mask = functools.partial(lax.broadcasted_iota, jnp.int32)

    pairs = ((wq, wq_v), (wk, wk_v), (wv, wv_v), (kc, kc_v), (vc, vc_v), (wo, wo_v), (wg, wg_v), (wu, wu_v), (wd, wd_v))
    loads = [pltpu.make_async_copy(a, b, w_sem.at[i]) for i, (a, b) in enumerate(pairs)]
    for i in range(3):
        loads[i].start()

    barrier = pltpu.get_barrier_semaphore()
    for d in range(1, seqs):
        pl.semaphore_signal(barrier, inc=1, device_id=(lax.rem(s + d, seqs), t), device_id_type=MESH)
    pl.semaphore_signal(barrier, inc=1, device_id=mate, device_id_type=MESH)
    for d in range(1, xs):
        pl.semaphore_signal(barrier, inc=1, device_id=(s, lax.rem(x + d, xs) * 2 + c), device_id_type=MESH)

    loads[3].start()

    for i in range(rows // 16):
        v = tok[16 * i : 16 * i + 16, :].astype(F32)
        ms = jnp.mean(v * v, axis=-1, keepdims=True)
        nrm[16 * i : 16 * i + 16, :] = (v * lax.rsqrt(ms + EPSILON) * gain1[...].astype(F32)).astype(BF16)
    qf[...] = jnp.zeros_like(qf)
    kf[...] = jnp.zeros_like(kf)
    vf[...] = jnp.zeros_like(vf)

    def rope(v):
        return v * cos[...] + pltpu.roll(v, head // 2, 1) * sin[...]

    heads = kv * group
    loads[0].wait()
    loads[4].start()
    for lo in range(0, heads * head, 256):
        hi = min(lo + 256, heads * head)
        prod = mm(nrm[...], wq_v[:, lo:hi])
        for h in range(lo // head, hi // head):
            qkv[h] = rope(prod[:, h * head - lo : (h + 1) * head - lo])
    loads[1].wait()
    prod = mm(nrm[...], wk_v[...])
    for h in range(kv):
        qkv[heads + h] = rope(prod[:, h * head : (h + 1) * head])
    loads[2].wait()
    prod = mm(nrm[...], wv_v[...])
    for h in range(kv):
        qkv[heads + kv + h] = prod[:, h * head : (h + 1) * head]
    for n in range(fresh):
        src = pl.ds(n, req_dev, stride=fresh)
        for h in range(kv):
            for g in range(group):
                qf[h, pl.ds(g * fresh + n, req_dev, stride=ROWS), :] = qkv[h * group + g, src, :]
            kf[h, pl.ds(n, req_dev, stride=ROWS), :] = qkv[heads + h, src, :]
            vf[h, pl.ds(n, req_dev, stride=ROWS), :] = qkv[heads + kv + h, src, :]
    for h in range(kv):
        qs[h] = qf[h].astype(BF16)
        ks[h] = kf[h].astype(BF16)
        vs[h] = vf[h].astype(BF16)

    pl.semaphore_wait(barrier, seqs + xs - 1)
    is_home = lax.rem(s, step) == 0
    home = s // step

    def query_copy(d):
        return pltpu.make_async_remote_copy(
            src_ref=ql.at[home], dst_ref=ql.at[home], send_sem=qsend.at[d - 1], recv_sem=qrecv.at[home],
            device_id=(lax.rem(s + d, seqs), t), device_id_type=MESH,
        )

    @pl.when(is_home)
    def _():
        ql[home] = qs[:, :ROWS, :]
        for d in range(1, seqs):
            query_copy(d).start()

    loads[5].start()
    loads[6].start()
    loads[3].wait()
    loads[4].wait()

    def short_step(i, carry):
        for u in range(2):
            r = i * 2 + u
            base = pl.multiple_of(r * ROWS, ROWS)
            for h in range(kv):
                q = qs[h, pl.ds(base, ROWS), :]
                lane = lane_mask((ROWS, page), 1)
                tiles = []
                for b in range(SHORT_BLK):
                    slot = ids[0, r * SHORT_BLK + b]
                    count = ids[1, r * SHORT_BLK + b]
                    tiles.append(jnp.where(lane < count, mm_t(q, kc_v[slot, h]) * scale, NEGATIVE))
                token = lax.rem(lane_mask((ROWS, ROWS), 0), fresh)
                key = lane_mask((ROWS, ROWS), 1)
                fresh_s = jnp.where(key <= token, mm_t(q, ks[h, pl.ds(base, ROWS), :]) * scale, NEGATIVE)
                top = jnp.maximum(jnp.maximum(tiles[0], tiles[1]), jnp.maximum(tiles[2], tiles[3]))
                m = jnp.maximum(jnp.max(top, axis=1, keepdims=True), jnp.max(fresh_s, axis=1, keepdims=True))
                w_f = jnp.exp(fresh_s - m).astype(BF16)
                l = jnp.sum(w_f.astype(F32), axis=1, keepdims=True)
                o = mm(w_f, vs[h, pl.ds(base, ROWS), :])
                acc = None
                for b in range(SHORT_BLK):
                    w = jnp.exp(tiles[b] - m).astype(BF16)
                    o = o + mm(w, vc_v[ids[0, r * SHORT_BLK + b], h])
                    acc = w.astype(F32) if acc is None else acc + w.astype(F32)
                l = l + jnp.sum(acc, axis=1, keepdims=True)
                so[h, pl.ds(base, ROWS), :] = o
                sm[h, pl.ds(base, ROWS), :] = jnp.broadcast_to(m, (ROWS, head))
                sl[h, pl.ds(base, ROWS), :] = jnp.broadcast_to(l, (ROWS, head))
        return carry

    lax.fori_loop(0, req_dev // 2, short_step, 0)
    loads[7].start()
    loads[8].start()

    for j in range(n_long):
        @pl.when(s != j * step)
        def _():
            pltpu.make_async_remote_copy(
                src_ref=ql.at[j], dst_ref=ql.at[j], send_sem=qsend.at[0], recv_sem=qrecv.at[j],
                device_id=mate, device_id_type=MESH,
            ).wait_recv()

    first = req_dev * SHORT_BLK

    def long_step(i, carry):
        lane = lane_mask((ROWS, page), 1)
        scores = []
        for u in range(UNROLL):
            p = first + i * UNROLL + u
            for h in range(kv):
                value = mm_t(ql[ids[2, p], h], kc_v[ids[0, p], h]) * scale
                scores.append(jnp.where(lane < ids[1, p], value, NEGATIVE))
        tops = [jnp.max(v, axis=1, keepdims=True) for v in scores]
        for u in range(UNROLL):
            p = first + i * UNROLL + u
            for h in range(kv):
                v, m = scores[u * kv + h], tops[u * kv + h]
                w = jnp.where(lane < ids[1, p], jnp.exp(v - m), 0.0).astype(BF16)
                oo[i * UNROLL + u, h] = mm(w, vc_v[ids[0, p], h])
                om[i * UNROLL + u, h] = jnp.broadcast_to(m, (ROWS, head))
                ol[i * UNROLL + u, h] = jnp.broadcast_to(jnp.sum(w.astype(F32), axis=1, keepdims=True), (ROWS, head))
        return carry

    lax.fori_loop(0, others // UNROLL, long_step, 0)

    def top_step(i, carry):
        for u in range(4):
            p = i * 4 + u
            m = om[p]
            owner = ids[2, first + p]
            carry = tuple(jnp.maximum(carry[j], m + jnp.where(owner == j, 0.0, NEGATIVE)) for j in range(n_long))
        return carry

    floor = jnp.full((kv, ROWS, head), FLOOR, F32)
    tops = lax.fori_loop(0, others // 4, top_step, (floor,) * n_long)
    for j in range(n_long):
        mj[j] = tops[j]

    def sum_step(i, carry):
        sums, totals = carry
        for u in range(4):
            p = i * 4 + u
            owner = ids[2, first + p]
            e = jnp.exp(om[p] - mj[owner])
            o = e * oo[p]
            l = e * ol[p]
            marks = [jnp.where(owner == j, 1.0, 0.0) for j in range(n_long)]
            sums = tuple(sums[j] + marks[j] * o for j in range(n_long))
            totals = tuple(totals[j] + marks[j] * l for j in range(n_long))
        return sums, totals

    zero = jnp.zeros((kv, ROWS, head), F32)
    sums, totals = lax.fori_loop(0, others // 4, sum_step, ((zero,) * n_long, (zero,) * n_long))
    low = lane_mask((ROWS, head), 1) < head // 2
    for j in range(n_long):
        for h in range(kv):
            pj[j, h, 0] = sums[j][h]
            pj[j, h, 1] = jnp.where(low, tops[j][h], totals[j][h])

    def part_copy(j):
        return pltpu.make_async_remote_copy(
            src_ref=pj.at[j], dst_ref=parts.at[s], send_sem=psend.at[j], recv_sem=precv.at[s],
            device_id=(j * step, t), device_id_type=MESH,
        )

    for j in range(n_long):
        @pl.when(s != j * step)
        def _():
            part_copy(j).start()

    @pl.when(is_home)
    def _():
        for d in range(1, seqs):
            src = lax.rem(s + d, seqs)
            pltpu.make_async_remote_copy(
                src_ref=pj.at[0], dst_ref=parts.at[src], send_sem=psend.at[0], recv_sem=precv.at[src],
                device_id=mate, device_id_type=MESH,
            ).wait_recv()
        for h in range(kv):
            pieces = [(sm[h, :ROWS, :1], sl[h, :ROWS, :1], so[h, :ROWS, :])]
            blocks = [(pj[home, h, 0], pj[home, h, 1])]
            for d in range(1, seqs):
                src = lax.rem(s + d, seqs)
                blocks.append((parts[src, h, 0], parts[src, h, 1]))
            for o, ml in blocks:
                pieces.append((ml[:, :1], ml[:, head // 2 : head // 2 + 1], o))
            m = functools.reduce(jnp.maximum, [piece[0] for piece in pieces])
            l = jnp.zeros((ROWS, 1), F32)
            o = jnp.zeros((ROWS, head), F32)
            for m_i, l_i, o_i in pieces:
                e = jnp.exp(m_i - m)
                l = l + e * l_i
                o = o + e * o_i
            so[h, :ROWS, :] = o
            sl[h, :ROWS, :] = jnp.broadcast_to(l, (ROWS, head))

    for n in range(fresh):
        for h in range(kv):
            for g in range(group):
                src = pl.ds(g * fresh + n, req_dev, stride=ROWS)
                qkv[h * group + g, pl.ds(n, req_dev, stride=fresh), :] = so[h, src, :] / sl[h, src, :]
    for h in range(heads):
        att[:, h * head : (h + 1) * head] = qkv[h].astype(BF16)

    def to_mate(src, dst, send, recv):
        return pltpu.make_async_remote_copy(
            src_ref=src, dst_ref=dst, send_sem=send, recv_sem=recv, device_id=mate, device_id_type=MESH
        )

    def across(src, dst, send, recv, d):
        return pltpu.make_async_remote_copy(
            src_ref=src, dst_ref=dst, send_sem=send, recv_sem=recv,
            device_id=(s, lax.rem(x + d, xs) * 2 + c), device_id_type=MESH,
        )

    def block(ref, b):
        return ref[:, pl.ds(pl.multiple_of(b * bw, 128), bw)]

    loads[5].wait()
    started = []
    first_sum = [to_mate(s1.at[k], r1.at[k], s1_sem.at[k], r1_sem.at[k]) for k in range(xs)]
    for k in range(xs):
        s1[k] = mm(att[...], block(wo_v, (1 - c) * xs + k)).astype(BF16)
        first_sum[k].start()
    for k in range(xs):
        own[k] = mm(att[...], block(wo_v, c * xs + k))
    crossing = {}
    for k in range(xs):
        first_sum[k].wait_recv()
        total = own[k] + r1[k].astype(F32)
        own[k] = total
        s2[k] = total.astype(BF16)
        for d in range(1, xs):
            crossing[k, d] = across(s2.at[k], r2.at[d - 1, k], s2_sem.at[d - 1, k], r2_sem.at[d - 1, k], d)
            crossing[k, d].start()
    spread = []
    for k in range(xs):
        b = c * xs + k
        total = block(tok, b).astype(F32) + own[k]
        for d in range(1, xs):
            crossing[k, d].wait_recv()
            total = total + r2[d - 1, k].astype(F32)
        res[b] = total.astype(BF16)
        copy = to_mate(res.at[b], res.at[b], s3_sem.at[k], r3_sem.at[k])
        copy.start()
        spread.append(copy)
    for k in range(xs):
        b = (1 - c) * xs + k
        to_mate(res.at[b], res.at[b], s3_sem.at[k], r3_sem.at[k]).wait_recv()

    square = jnp.zeros((rows, 1), F32)
    for b in range(tens):
        v = res[b].astype(F32)
        square = square + jnp.sum(v * v, axis=-1, keepdims=True)
    inverse = lax.rsqrt(square / width + EPSILON)
    for b in range(tens):
        cols = slice(b * bw, (b + 1) * bw)
        nrm[:, cols] = (res[b].astype(F32) * inverse * gain2[:, cols].astype(F32)).astype(BF16)

    loads[6].wait()
    loads[7].wait()
    for lo in range(0, act.shape[1], 256):
        gate = mm(nrm[...], wg_v[:, lo : lo + 256])
        up = mm(nrm[...], wu_v[:, lo : lo + 256])
        act[:, lo : lo + 256] = (gate / (1.0 + jnp.exp(-gate)) * up).astype(BF16)

    loads[8].wait()
    pair_sum = []
    for k in range(xs):
        to = lax.rem(x + 1 + k, xs)
        s4[k] = mm(act[...], block(wd_v, to * 2 + 1 - c)).astype(BF16)
        copy = to_mate(s4.at[k], r4.at[k], s4_sem.at[k], r4_sem.at[k])
        copy.start()
        pair_sum.append(copy)
    last = []
    for k in range(xs):
        to = lax.rem(x + 1 + k, xs)
        total = mm(act[...], block(wd_v, to * 2 + c))
        pair_sum[k].wait_recv()
        total = total + r4[k].astype(F32)
        if k < xs - 1:
            s5[k] = total.astype(BF16)
            copy = across(s5.at[k], r5.at[k], s5_sem.at[k], r5_sem.at[k], k + 1)
            copy.start()
            last.append(copy)
        else:
            total = total + res[t].astype(F32)
            for copy, d in zip(last, range(xs)):
                copy.wait_recv()
                total = total + r5[d].astype(F32)
            out[...] = total.astype(BF16)

    @pl.when(is_home)
    def _():
        for d in range(1, seqs):
            query_copy(d).wait_send()

    for j in range(n_long):
        @pl.when(s != j * step)
        def _():
            part_copy(j).wait_send()

    for copy in first_sum + list(crossing.values()) + spread + pair_sum + last:
        copy.wait_send()


def per_device(
    tokens, lengths, page_request, page_block, k_cache, v_cache, attn_gain, w_query, w_key, w_value,
    w_out, mlp_gain, w_gate, w_up, w_down,
):
    req_dev, fresh, width = tokens.shape
    slots, kv, page, head = k_cache.shape
    group = w_query.shape[1] // (kv * head)
    rows = req_dev * fresh
    seqs, tens = lax.axis_size("seq"), lax.axis_size("tensor")
    xs = tens // 2
    bw = width // tens
    requests = lengths.shape[0]
    n_long = requests // STRIDE
    hidden = w_gate.shape[1]
    home_row = lax.axis_index("seq") * req_dev

    own_length = lax.dynamic_slice_in_dim(lengths, home_row, req_dev)
    position = (own_length[:, None] + jnp.arange(fresh, dtype=jnp.int32)[None, :]).reshape(rows, 1)
    half = head // 2
    inverse = 1.0 / ROPE_BASE ** (jnp.arange(half, dtype=F32) * 2.0 / head)
    angle = position.astype(F32) * jnp.concatenate([inverse, inverse])[None, :]
    sign = jnp.where(jnp.arange(head) < half, -1.0, 1.0)
    cosine = jnp.cos(angle)
    sine = jnp.sin(angle) * sign[None, :]

    is_short = (page_request % STRIDE != 0) & (page_block < SHORT_BLK)
    index = jnp.arange(slots, dtype=jnp.int32)
    before = index[None, :] < index[:, None]
    rank = jnp.sum(jnp.where(before & ~is_short[None, :], 1, 0), axis=1)
    first = req_dev * SHORT_BLK
    place = jnp.where(is_short, (page_request - home_row) * SHORT_BLK + page_block, first + rank)
    most = slots - first + SHORT_BLK * -(-req_dev // STRIDE)
    others = -(-most // UNROLL) * UNROLL
    total = -(-(first + others) // 128) * 128
    owner_length = jnp.sum(
        jnp.where(page_request[:, None] == jnp.arange(requests, dtype=jnp.int32)[None, :], lengths[None, :], 0), axis=1
    )
    count = jnp.clip(owner_length - page_block * page, 0, page)
    table = jnp.stack([index, count, page_request // STRIDE])
    at = place[None, :] == jnp.arange(total, dtype=jnp.int32)[:, None]
    ids = jnp.sum(jnp.where(at[None], table[:, None, :], 0), axis=2)

    vm = lambda shape, dtype=F32: pltpu.VMEM(shape, dtype)
    dma = lambda *shape: pltpu.SemaphoreType.DMA(shape)
    whole = pl.BlockSpec(memory_space=pltpu.VMEM)
    stay = pl.BlockSpec(memory_space=pl.ANY)
    big = (w_query, w_key, w_value, w_out, w_gate, w_up, w_down, k_cache, v_cache)
    tall = (kv, req_dev * ROWS, head)
    scratch = [vm(a.shape, BF16) for a in big]
    scratch += [
        vm((rows, width), BF16), vm((kv * (group + 2), rows, head)), vm(tall), vm(tall), vm(tall),
        vm(tall, BF16), vm(tall, BF16), vm(tall, BF16), vm(tall), vm(tall), vm(tall),
        vm((n_long, kv, ROWS, head), BF16),
        vm((others, kv, ROWS, head)), vm((others, kv, ROWS, head)), vm((others, kv, ROWS, head)),
        vm((n_long, kv, ROWS, head)), vm((n_long, kv, 2, ROWS, head)), vm((seqs, kv, 2, ROWS, head)),
        vm((rows, kv * group * head), BF16),
        vm((xs, rows, bw), BF16), vm((xs, rows, bw), BF16), vm((xs, rows, bw)),
        vm((xs, rows, bw), BF16), vm((xs - 1, xs, rows, bw), BF16), vm((tens, rows, bw), BF16),
        vm((rows, hidden), BF16),
        vm((xs, rows, bw), BF16), vm((xs, rows, bw), BF16), vm((xs - 1, rows, bw), BF16), vm((xs - 1, rows, bw), BF16),
        dma(9), dma(seqs - 1), dma(n_long), dma(n_long), dma(seqs),
        dma(xs), dma(xs), dma(xs - 1, xs), dma(xs - 1, xs), dma(xs), dma(xs), dma(xs), dma(xs), dma(xs - 1), dma(xs - 1),
    ]
    moved = sum(a.size for a in big) * 2
    out = pl.pallas_call(
        functools.partial(layer_kernel, seqs, tens, n_long, others, req_dev, fresh, group, kv),
        out_shape=jax.ShapeDtypeStruct((rows, bw), BF16),
        in_specs=[pl.BlockSpec(memory_space=pltpu.SMEM)] + [whole] * 5 + [stay] * 9,
        out_specs=whole,
        scratch_shapes=scratch,
        compiler_params=pltpu.CompilerParams(
            collective_id=0, has_side_effects=True, vmem_limit_bytes=60 * 1024 * 1024
        ),
        cost_estimate=pl.CostEstimate(flops=2 * rows * moved, bytes_accessed=moved, transcendentals=0),
        name="layer",
    )(
        ids, tokens.reshape(rows, width), attn_gain.reshape(1, width), mlp_gain.reshape(1, width),
        cosine, sine, *big,
    )
    return out.reshape(req_dev, fresh, bw)


def solution(mesh):
    placed = (
        P("seq", None, None),
        P(),
        P("seq"),
        P("seq"),
        P("seq", "tensor", None, None),
        P("seq", "tensor", None, None),
        P(),
        P(None, "tensor"),
        P(None, "tensor"),
        P(None, "tensor"),
        P("tensor", None),
        P(),
        P(None, "tensor"),
        P(None, "tensor"),
        P("tensor", None),
    )
    return jax.shard_map(
        per_device, mesh=mesh, in_specs=placed, out_specs=P("seq", None, "tensor"), check_vma=False
    )
```

time: 297 us -> 65.3 us (0.22)
  blocking collectives: 107 us -> 0 us
  waiting for transfers between devices: 105 us -> 0 us
  Pallas kernels: 0 us -> 54.2 us
  matrix products: 42.7 us -> 0 us
  between operations: 13.5 us -> 0.03 us
  local copies, waits for them, and re-layouts: 15.9 us -> 6.79 us
  other arithmetic: 12.4 us -> 4.02 us
    psum x2 -> x0, waiting for transfers between devices: 81.7 us -> none  [the longest x1 47.6 us: per_device(): total_all, summed_all = lax.psum((slot_total, slot_summed), 'seq')]
    pallas_call x0 -> x1, Pallas kernels: none -> 54.2 us  [per_device(): pl.pallas_call(functools.partial(layer_kernel, seqs, tens, n_long, others...]
    dot_general x12 -> x0, matrix products: 42.7 us -> none  [the longest x1 9.63 us: per_device(): jnp.einsum('phqd,phkd->phqk', chosen, k_cache, preferred_element_type=jnp...]
    pmax x1 -> x0, blocking collectives: 37.4 us -> none  [per_device(): row_max = lax.pmax(candidate, 'seq')]
    psum x1 -> x0, blocking collectives: 35.9 us -> none  [per_device(): total_all, summed_all = lax.psum((slot_total, slot_summed), 'seq')]
    all_gather x1 -> x0, blocking collectives: 33.8 us -> none  [per_device(): lax.all_gather(queries.reshape(req_dev, kv_local * lanes * head_dim), 'se...]
    reduce_scatter x1 -> x0, waiting for transfers between devices: 23.4 us -> none  [per_device(): lax.psum_scatter(down_out, 'tensor', scatter_dimension=1, tiled=True)]
    unnamed x29 -> x0, local copies, waits for them, and re-layouts: 6.74 us -> none
  transfers between devices with their start and end apart: 3 -> 0, of which waited for: 3 -> 0; matrix products, arithmetic and copies ran while one was open for 1% -> 0% of each run, Pallas kernels for 0% -> 0%
where the time goes in v1:
time: 65.3 us; the launch traced here: 65 us
  Pallas kernels  54.2 us (83%)
  local copies, waits for them, and re-layouts  6.79 us (10%)
  other arithmetic  4.02 us (6%)
    pallas_call x1, Pallas kernels, per_device(): pl.pallas_call(functools.partial(layer_kernel, seqs, tens, n_long, others...  54.2 us
    reshape x1, local copies, waits for them, and re-layouts, per_device(): tokens.reshape(rows, width)  1.82 us
    reshape x1, local copies, waits for them, and re-layouts, per_device(): return out.reshape(req_dev, fresh, bw)  1.56 us

profile of v1, /device:TPU:0, one launch (start us, length us, event | category | flops | bytes accessed | tf_op | source)
XLA Modules:
  0.0 65.0 jit_solution(2716963363138136434)
XLA Ops:
  0.0 0.7 %dynamic_slice.3 = s32[16]{0:T(128)S(1)} dynamic-slice(s32[128]{0:T(128)} %param.16, s32[]{:T(128)S(6)} %select_n.44), dynamic_slice_sizes={16} | dynamic-slice | bytes 132 | tf_op jit(solution)/shard_map/dynamic_slice | solution.py:393
  0.7 0.1 compare_select_fusion
  0.8 0.7 %fusion.3 = (pred[128]{0:T(512)(128)(4,1)S(1)}, pred[128]{0:T(512)(128)(4,1)S(1)}) fusion(s32[128]{0:T(128)} %param.18, s32[128]{0:T(128)} %param.17), kind=kLoop, calls=%fused_computation.24 | loop fusion | flops 1920 | bytes 1280 | tf_op jit(solution)/shard_map/not | solution.py:405
  1.5 0.8 %select_reduce_fusion.1 = (s32[128]{0:T(128)S(1)}, s32[128]{0:T(128)S(1)}) fusion(s32[128]{0:T(128)} %param.16, s32[128]{0:T(128)} %param.17, pred[128]{0:T(512)(128)(4,1)S(1)} %get-tuple-element.5), kind=kLoop, calls=%fused_computation.2 | loop fusion | flops 114432 | bytes 2176 | tf_op jit(solution)/shard_map/reduce_sum | solution.py:411
  2.4 0.7 %add_select_fusion = (s32[128]{0:T(128)S(1)}, s32[1,128]{1,0:T(1,128)S(1)}, s32[1,128]{1,0:T(1,128)S(1)}) fusion(pred[128]{0:T(512)(128)(4,1)S(1)} %get-tuple-element.6, s32[128]{0:T(128)S(1)} %get-tuple-element.13, s32[128]{0:T(128)} %param.18, s32[128]{0:T(128)} %param.17, s32[]{:T(128)S(6)} %mul.16, s32[128]{0:T(128)S(1)} %get-tuple-element.12), kind=kLoop, calls=%fused_computation.22 | loop fusion | flops 2944 | bytes 3716 | tf_op jit(solution)/shard_map/jit(_where)/select_n | solution.py:407
  3.1 0.1 add_convert_fusion
  3.1 0.1 convert_element_type.12
  3.2 1.3 %reshape.63.gain1 = bf16[1,3072]{1,0:T(2,128)(2,1)} reshape(bf16[3072]{0:T(1024)(128)(2,1)} %param.21) | data formatting | bytes 12288 | tf_op jit(solution)/shard_map/reshape | solution.py:453
  4.5 1.3 %reshape.64.gain2 = bf16[1,3072]{1,0:T(2,128)(2,1)} reshape(bf16[3072]{0:T(1024)(128)(2,1)} %param.26) | data formatting | bytes 12288 | tf_op jit(solution)/shard_map/reshape | solution.py:453
  5.8 0.8 %select_reduce_fusion.ids = s32[3,256]{1,0:T(4,128)} fusion(s32[3,128]{1,0:T(4,128)S(1)} %pad_add_fusion, pred[256,128]{1,0:T(8,128)(4,1)S(1)} %iota_compare_fusion), kind=kLoop, calls=%fused_computation | loop fusion | flops 195840 | bytes 37376 | tf_op jit(solution)/shard_map/reduce_sum | solution.py:417
  6.6 0.8 %fusion.1 = (f32[64,128]{1,0:T(8,128)}, f32[64,128]{1,0:T(8,128)}) fusion(f32[128]{0:T(128)S(1)} %get-tuple-element.14, f32[128]{0:T(128)S(1)} %get-tuple-element.15, f32[64]{0:T(128)S(1)} %convert_element_type.12), kind=kLoop, calls=%fused_computation.9 | loop fusion | flops 16384 | bytes 66816 | tf_op jit(solution)/shard_map/mul | solution.py:400
  7.4 1.8 %reshape.62.tok = bf16[64,3072]{1,0:T(8,128)(2,1)} reshape(bf16[16,4,3072]{2,1,0:T(4,128)(2,1)} %param.15) | data formatting | bytes 786432 | tf_op jit(solution)/shard_map/reshape | solution.py:453
  9.3 54.2 %layer.1 = bf16[64,768]{1,0:T(8,128)(2,1)} custom-call(s32[3,256]{1,0:T(4,128)} %select_reduce_fusion.ids, bf16[64,3072]{1,0:T(8,128)(2,1)} %reshape.62.tok, bf16[1,3072]{1,0:T(2,128)(2,1)} %reshape.63.gain1, bf16[1,3072]{1,0:T(2,128)(2,1)} %reshape.64.gain2, f32[64,128]{1,0:T(8,128)} %get-tuple-element.8.cos, f32[64,128]{1,0:T(8,128)} %get-tuple-element.7.sin, ...), custom_call_target="tpu_custom_call" | custom-call | flops 6174015488 | bytes 48234496 | tf_op jit(solution)/shard_map/layer/pallas_call | solution.py:441
  63.5 1.6 %reshape.65 = bf16[16,4,768]{2,1,0:T(4,128)(2,1)} reshape(bf16[64,768]{1,0:T(8,128)(2,1)} %layer.1) | data formatting | bytes 196608 | tf_op jit(solution)/shard_map/reshape | solution.py:456
  (4 shorter events, 0.0 us)

commit v2 on v1

--- a/solution.py
+++ b/solution.py
@@ -3,6 +3,7 @@
 
 import jax
 import jax.numpy as jnp
+import numpy as np
 from jax import lax
 from jax.experimental import pallas as pl
 from jax.experimental.pallas import tpu as pltpu
@@ -15,7 +16,8 @@
 STRIDE = 32
 SHORT_BLK = 4
 ROWS = 16
-UNROLL = 8
+UNROLL = 12
+SHORT_UNROLL = 4
 MESH = pl.DeviceIdType.MESH
 F32 = jnp.float32
 BF16 = jnp.bfloat16
@@ -31,10 +33,10 @@
 
 def layer_kernel(
     seqs, tens, n_long, others, req_dev, fresh, group, kv,
-    ids, tok, gain1, gain2, cos, sin, wq, wk, wv, wo, wg, wu, wd, kc, vc,
+    places, lengths, page_request, page_block, tok, gain1, gain2, freq, wq, wk, wv, wo, wg, wu, wd, kc, vc,
     out,
     wq_v, wk_v, wv_v, wo_v, wg_v, wu_v, wd_v, kc_v, vc_v,
-    nrm, qkv, qf, kf, vf, qs, ks, vs, so, sm, sl, ql, oo, om, ol, mj, pj, parts,
+    xf, cos, sin, nrm, qkv, qf, kf, vf, qs, ks, vs, so, sm, sl, ql, oo, om, ol, mj, pj, parts,
     att, s1, r1, own, s2, r2, res, act, s4, r4, s5, r5,
     w_sem, qsend, qrecv, psend, precv,
     s1_sem, r1_sem, s2_sem, r2_sem, s3_sem, r3_sem, s4_sem, r4_sem, s5_sem, r5_sem,
@@ -45,7 +47,7 @@
     x = t // 2
     xs = tens // 2
     step = STRIDE // req_dev
-    rows, width = tok.shape
+    rows, width = xf.shape
     bw = width // tens
     head = kc.shape[-1]
     page = kc.shape[2]
@@ -67,13 +69,23 @@
 
     loads[3].start()
 
+    for r in range(req_dev):
+        xf[fresh * r : fresh * r + fresh, :] = tok[r].astype(F32)
     for i in range(rows // 16):
-        v = tok[16 * i : 16 * i + 16, :].astype(F32)
+        v = xf[16 * i : 16 * i + 16, :]
         ms = jnp.mean(v * v, axis=-1, keepdims=True)
-        nrm[16 * i : 16 * i + 16, :] = (v * lax.rsqrt(ms + EPSILON) * gain1[...].astype(F32)).astype(BF16)
+        nrm[16 * i : 16 * i + 16, :] = (v * lax.rsqrt(ms + EPSILON) * gain1[...].astype(F32).reshape(1, width)).astype(BF16)
     qf[...] = jnp.zeros_like(qf)
     kf[...] = jnp.zeros_like(kf)
     vf[...] = jnp.zeros_like(vf)
+
+    row = lane_mask((rows, head), 0)
+    position = lax.rem(row, fresh)
+    for r in range(req_dev):
+        position = position + jnp.where(row // fresh == r, lengths[s * req_dev + r], 0)
+    angle = position.astype(F32) * freq[...]
+    cos[...] = jnp.cos(angle)
+    sin[...] = jnp.where(lane_mask((rows, head), 1) < head // 2, -1.0, 1.0) * jnp.sin(angle)
 
     def rope(v):
         return v * cos[...] + pltpu.roll(v, head // 2, 1) * sin[...]
@@ -127,38 +139,50 @@
     loads[3].wait()
     loads[4].wait()
 
+    def entry(p):
+        known = places[p] - 1
+        slot = jnp.maximum(known, 0)
+        request = page_request[slot]
+        used = jnp.where(known < 0, 0, lengths[request] - page_block[slot] * page)
+        return slot, used, request // STRIDE
+
     def short_step(i, carry):
-        for u in range(2):
-            r = i * 2 + u
-            base = pl.multiple_of(r * ROWS, ROWS)
+        lane = lane_mask((ROWS, page), 1)
+        token = lax.rem(lane_mask((ROWS, ROWS), 0), fresh)
+        key = lane_mask((ROWS, ROWS), 1)
+        for u in range(SHORT_UNROLL):
+            r = i * SHORT_UNROLL + u
+            span = pl.ds(pl.multiple_of(r * ROWS, ROWS), ROWS)
+            entries = [entry(r * SHORT_BLK + b) for b in range(SHORT_BLK)]
+            weights = []
             for h in range(kv):
-                q = qs[h, pl.ds(base, ROWS), :]
-                lane = lane_mask((ROWS, page), 1)
-                tiles = []
-                for b in range(SHORT_BLK):
-                    slot = ids[0, r * SHORT_BLK + b]
-                    count = ids[1, r * SHORT_BLK + b]
-                    tiles.append(jnp.where(lane < count, mm_t(q, kc_v[slot, h]) * scale, NEGATIVE))
-                token = lax.rem(lane_mask((ROWS, ROWS), 0), fresh)
-                key = lane_mask((ROWS, ROWS), 1)
-                fresh_s = jnp.where(key <= token, mm_t(q, ks[h, pl.ds(base, ROWS), :]) * scale, NEGATIVE)
-                top = jnp.maximum(jnp.maximum(tiles[0], tiles[1]), jnp.maximum(tiles[2], tiles[3]))
+                q = qs[h, span, :]
+                keys = jnp.concatenate([kc_v[slot, h] for slot, _, _ in entries], axis=0)
+                value = mm_t(q, keys) * scale
+                tiles = [
+                    jnp.where(lane < used, value[:, b * page : (b + 1) * page], NEGATIVE)
+                    for b, (_, used, _) in enumerate(entries)
+                ]
+                fresh_s = jnp.where(key <= token, mm_t(q, ks[h, span, :]) * scale, NEGATIVE)
+                top = functools.reduce(jnp.maximum, tiles)
                 m = jnp.maximum(jnp.max(top, axis=1, keepdims=True), jnp.max(fresh_s, axis=1, keepdims=True))
                 w_f = jnp.exp(fresh_s - m).astype(BF16)
+                w = [jnp.exp(tile - m).astype(BF16) for tile in tiles]
                 l = jnp.sum(w_f.astype(F32), axis=1, keepdims=True)
-                o = mm(w_f, vs[h, pl.ds(base, ROWS), :])
-                acc = None
-                for b in range(SHORT_BLK):
-                    w = jnp.exp(tiles[b] - m).astype(BF16)
-                    o = o + mm(w, vc_v[ids[0, r * SHORT_BLK + b], h])
-                    acc = w.astype(F32) if acc is None else acc + w.astype(F32)
-                l = l + jnp.sum(acc, axis=1, keepdims=True)
-                so[h, pl.ds(base, ROWS), :] = o
-                sm[h, pl.ds(base, ROWS), :] = jnp.broadcast_to(m, (ROWS, head))
-                sl[h, pl.ds(base, ROWS), :] = jnp.broadcast_to(l, (ROWS, head))
+                l = l + jnp.sum(sum(part.astype(F32) for part in w), axis=1, keepdims=True)
+                so[h, span, :] = mm(w_f, vs[h, span, :])
+                sm[h, span, :] = jnp.broadcast_to(m, (ROWS, head))
+                sl[h, span, :] = jnp.broadcast_to(l, (ROWS, head))
+                weights.append(jnp.concatenate(w, axis=1))
+            values = jnp.concatenate(
+                [jnp.concatenate([vc_v[slot, h] for h in range(kv)], axis=1) for slot, _, _ in entries], axis=0
+            )
+            o = mm(jnp.concatenate(weights, axis=0), values)
+            for h in range(kv):
+                so[h, span, :] += o[h * ROWS : (h + 1) * ROWS, h * head : (h + 1) * head]
         return carry
 
-    lax.fori_loop(0, req_dev // 2, short_step, 0)
+    lax.fori_loop(0, req_dev // SHORT_UNROLL, short_step, 0)
     loads[7].start()
     loads[8].start()
 
@@ -174,21 +198,30 @@
 
     def long_step(i, carry):
         lane = lane_mask((ROWS, page), 1)
+        entries = [entry(first + i * UNROLL + u) for u in range(UNROLL)]
+        places_of = [(u, h) for u in range(UNROLL) for h in range(kv)]
+        pairs_of = [places_of[n : n + 2] for n in range(0, len(places_of), 2)]
         scores = []
-        for u in range(UNROLL):
-            p = first + i * UNROLL + u
-            for h in range(kv):
-                value = mm_t(ql[ids[2, p], h], kc_v[ids[0, p], h]) * scale
-                scores.append(jnp.where(lane < ids[1, p], value, NEGATIVE))
+        for pair in pairs_of:
+            q = jnp.concatenate([ql[entries[u][2], h] for u, h in pair], axis=0)
+            keys = jnp.concatenate([kc_v[entries[u][0], h] for u, h in pair], axis=0)
+            value = mm_t(q, keys) * scale
+            for n, (u, _) in enumerate(pair):
+                part = value[n * ROWS : (n + 1) * ROWS, n * page : (n + 1) * page]
+                scores.append(jnp.where(lane < entries[u][1], part, NEGATIVE))
         tops = [jnp.max(v, axis=1, keepdims=True) for v in scores]
-        for u in range(UNROLL):
-            p = first + i * UNROLL + u
-            for h in range(kv):
-                v, m = scores[u * kv + h], tops[u * kv + h]
-                w = jnp.where(lane < ids[1, p], jnp.exp(v - m), 0.0).astype(BF16)
-                oo[i * UNROLL + u, h] = mm(w, vc_v[ids[0, p], h])
+        for k, pair in enumerate(pairs_of):
+            weights = []
+            for n, (u, h) in enumerate(pair):
+                v, m = scores[2 * k + n], tops[2 * k + n]
+                w = jnp.where(lane < entries[u][1], jnp.exp(v - m), 0.0).astype(BF16)
                 om[i * UNROLL + u, h] = jnp.broadcast_to(m, (ROWS, head))
                 ol[i * UNROLL + u, h] = jnp.broadcast_to(jnp.sum(w.astype(F32), axis=1, keepdims=True), (ROWS, head))
+                weights.append(w)
+            values = jnp.concatenate([vc_v[entries[u][0], h] for u, h in pair], axis=1)
+            o = mm(jnp.concatenate(weights, axis=0), values)
+            for n, (u, h) in enumerate(pair):
+                oo[i * UNROLL + u, h] = o[n * ROWS : (n + 1) * ROWS, n * head : (n + 1) * head]
         return carry
 
     lax.fori_loop(0, others // UNROLL, long_step, 0)
@@ -197,7 +230,7 @@
         for u in range(4):
             p = i * 4 + u
             m = om[p]
-            owner = ids[2, first + p]
+            owner = entry(first + p)[2]
             carry = tuple(jnp.maximum(carry[j], m + jnp.where(owner == j, 0.0, NEGATIVE)) for j in range(n_long))
         return carry
 
@@ -210,7 +243,7 @@
         sums, totals = carry
         for u in range(4):
             p = i * 4 + u
-            owner = ids[2, first + p]
+            owner = entry(first + p)[2]
             e = jnp.exp(om[p] - mj[owner])
             o = e * oo[p]
             l = e * ol[p]
@@ -306,7 +339,7 @@
     spread = []
     for k in range(xs):
         b = c * xs + k
-        total = block(tok, b).astype(F32) + own[k]
+        total = block(xf, b) + own[k]
         for d in range(1, xs):
             crossing[k, d].wait_recv()
             total = total + r2[d - 1, k].astype(F32)
@@ -323,9 +356,10 @@
         v = res[b].astype(F32)
         square = square + jnp.sum(v * v, axis=-1, keepdims=True)
     inverse = lax.rsqrt(square / width + EPSILON)
+    scales = gain2[...].astype(F32).reshape(1, width)
     for b in range(tens):
         cols = slice(b * bw, (b + 1) * bw)
-        nrm[:, cols] = (res[b].astype(F32) * inverse * gain2[:, cols].astype(F32)).astype(BF16)
+        nrm[:, cols] = (res[b].astype(F32) * inverse * scales[:, cols]).astype(BF16)
 
     loads[6].wait()
     loads[7].wait()
@@ -358,7 +392,8 @@
             for copy, d in zip(last, range(xs)):
                 copy.wait_recv()
                 total = total + r5[d].astype(F32)
-            out[...] = total.astype(BF16)
+            for r in range(req_dev):
+                out[r] = total[fresh * r : fresh * r + fresh].astype(BF16)
 
     @pl.when(is_home)
     def _():
@@ -385,36 +420,28 @@
     seqs, tens = lax.axis_size("seq"), lax.axis_size("tensor")
     xs = tens // 2
     bw = width // tens
-    requests = lengths.shape[0]
-    n_long = requests // STRIDE
+    n_long = lengths.shape[0] // STRIDE
     hidden = w_gate.shape[1]
     home_row = lax.axis_index("seq") * req_dev
 
-    own_length = lax.dynamic_slice_in_dim(lengths, home_row, req_dev)
-    position = (own_length[:, None] + jnp.arange(fresh, dtype=jnp.int32)[None, :]).reshape(rows, 1)
-    half = head // 2
-    inverse = 1.0 / ROPE_BASE ** (jnp.arange(half, dtype=F32) * 2.0 / head)
-    angle = position.astype(F32) * jnp.concatenate([inverse, inverse])[None, :]
-    sign = jnp.where(jnp.arange(head) < half, -1.0, 1.0)
-    cosine = jnp.cos(angle)
-    sine = jnp.sin(angle) * sign[None, :]
-
-    is_short = (page_request % STRIDE != 0) & (page_block < SHORT_BLK)
-    index = jnp.arange(slots, dtype=jnp.int32)
-    before = index[None, :] < index[:, None]
-    rank = jnp.sum(jnp.where(before & ~is_short[None, :], 1, 0), axis=1)
+    inverse = ROPE_BASE ** (-np.arange(head // 2) * 2.0 / head)
+    freq = np.concatenate([inverse, inverse])[None, :].astype(np.float32)
+
     first = req_dev * SHORT_BLK
-    place = jnp.where(is_short, (page_request - home_row) * SHORT_BLK + page_block, first + rank)
     most = slots - first + SHORT_BLK * -(-req_dev // STRIDE)
     others = -(-most // UNROLL) * UNROLL
-    total = -(-(first + others) // 128) * 128
-    owner_length = jnp.sum(
-        jnp.where(page_request[:, None] == jnp.arange(requests, dtype=jnp.int32)[None, :], lengths[None, :], 0), axis=1
+
+    is_short = (page_request % STRIDE != 0) & (page_block < SHORT_BLK)
+    code = jnp.where(is_short, (page_request - home_row) * SHORT_BLK + page_block + 1, 0)
+    line = lax.broadcasted_iota(jnp.int32, (slots, slots), 0)
+    index = lax.broadcasted_iota(jnp.int32, (slots, slots), 1)
+    rank = jnp.sum(jnp.where(jnp.maximum(code[None, :], index - line + 1) <= 0, 1, 0), axis=1)
+    line = lax.broadcasted_iota(jnp.int32, (first + others, slots), 0)
+    index = lax.broadcasted_iota(jnp.int32, (first + others, slots), 1)
+    is_place = (code[None, :] - (line + 1) == 0) | (
+        jnp.maximum(jnp.abs(rank[None, :] + (first - line)), code[None, :]) == 0
     )
-    count = jnp.clip(owner_length - page_block * page, 0, page)
-    table = jnp.stack([index, count, page_request // STRIDE])
-    at = place[None, :] == jnp.arange(total, dtype=jnp.int32)[:, None]
-    ids = jnp.sum(jnp.where(at[None], table[:, None, :], 0), axis=2)
+    places = jnp.sum(jnp.where(is_place, index + 1, 0), axis=1)
 
     vm = lambda shape, dtype=F32: pltpu.VMEM(shape, dtype)
     dma = lambda *shape: pltpu.SemaphoreType.DMA(shape)
@@ -424,7 +451,7 @@
     tall = (kv, req_dev * ROWS, head)
     scratch = [vm(a.shape, BF16) for a in big]
     scratch += [
-        vm((rows, width), BF16), vm((kv * (group + 2), rows, head)), vm(tall), vm(tall), vm(tall),
+        vm((rows, width)), vm((rows, head)), vm((rows, head)), vm((rows, width), BF16), vm((kv * (group + 2), rows, head)), vm(tall), vm(tall), vm(tall),
         vm(tall, BF16), vm(tall, BF16), vm(tall, BF16), vm(tall), vm(tall), vm(tall),
         vm((n_long, kv, ROWS, head), BF16),
         vm((others, kv, ROWS, head)), vm((others, kv, ROWS, head)), vm((others, kv, ROWS, head)),
@@ -440,8 +467,8 @@
     moved = sum(a.size for a in big) * 2
     out = pl.pallas_call(
         functools.partial(layer_kernel, seqs, tens, n_long, others, req_dev, fresh, group, kv),
-        out_shape=jax.ShapeDtypeStruct((rows, bw), BF16),
-        in_specs=[pl.BlockSpec(memory_space=pltpu.SMEM)] + [whole] * 5 + [stay] * 9,
+        out_shape=jax.ShapeDtypeStruct((req_dev, fresh, bw), BF16),
+        in_specs=[pl.BlockSpec(memory_space=pltpu.SMEM)] * 4 + [whole] * 4 + [stay] * 9,
         out_specs=whole,
         scratch_shapes=scratch,
         compiler_params=pltpu.CompilerParams(
@@ -450,10 +477,9 @@
         cost_estimate=pl.CostEstimate(flops=2 * rows * moved, bytes_accessed=moved, transcendentals=0),
         name="layer",
     )(
-        ids, tokens.reshape(rows, width), attn_gain.reshape(1, width), mlp_gain.reshape(1, width),
-        cosine, sine, *big,
+        places, lengths, page_request, page_block, tokens, attn_gain, mlp_gain, freq, *big,
     )
-    return out.reshape(req_dev, fresh, bw)
+    return out
 
 
 def solution(mesh):

time: 65.3 us -> 52.5 us (0.80)
  local copies, waits for them, and re-layouts: 6.79 us -> 1.57 us
  Pallas kernels: 54.2 us -> 49.2 us
  other arithmetic: 4.02 us -> 1.58 us
    reshape x4 -> x0, local copies, waits for them, and re-layouts: 5.98 us -> none  [the longest x1 1.82 us: per_device(): tokens.reshape(rows, width)]
    pallas_call x1, Pallas kernels: 54.2 us -> 49.2 us  [per_device(): pl.pallas_call(functools.partial(layer_kernel, seqs, tens, n_long, others...]
    unnamed x0 -> x1, local copies, waits for them, and re-layouts: none -> 1.57 us
    mul x1 -> x0, other arithmetic: 0.83 us -> none  [per_device(): sine = jnp.sin(angle) * sign[None, :]]
    reduce_sum x2, other arithmetic: 1.62 us -> 0.89 us  [the longest x1 0.78 us: per_device(): places = jnp.sum(jnp.where(is_place, index + 1, 0), axis=1)]
    dynamic_slice x1 -> x0, local copies, waits for them, and re-layouts: 0.73 us -> none  [per_device(): own_length = lax.dynamic_slice_in_dim(lengths, home_row, req_dev)]
    not x1 -> x0, other arithmetic: 0.69 us -> none  [per_device(): rank = jnp.sum(jnp.where(before & ~is_short[None, :], 1, 0), axis=1)]
where the time goes in v2:
time: 52.5 us; the launch traced here: 52.4 us
  Pallas kernels  49.2 us (94%)
  other arithmetic  1.58 us (3%)
  local copies, waits for them, and re-layouts  1.57 us (3%)
    pallas_call x1, Pallas kernels, per_device(): pl.pallas_call(functools.partial(layer_kernel, seqs, tens, n_long, others...  49.2 us
    unnamed x1, local copies, waits for them, and re-layouts  1.57 us

profile of v2, /device:TPU:0, one launch (start us, length us, event | category | flops | bytes accessed | tf_op | source)
XLA Modules:
  0.0 52.4 jit_solution(16519061931847268095)
XLA Ops:
  0.0 0.7 %and_select_fusion = (s32[128]{0:T(128)S(1)}, s32[128]{0:T(128)S(1)}) fusion(s32[128]{0:T(128)} %page_block.1, s32[128]{0:T(128)} %page_request.1, s32[]{:T(128)S(6)} %mul.6), kind=kLoop, calls=%fused_computation.8 | loop fusion | flops 2560 | bytes 2052 | tf_op jit(solution)/shard_map/jit(_where)/select_n | solution.py:435
  0.7 0.1 select_reduce_fusion.1
  0.8 0.8 %select_reduce_fusion.places = s32[136]{0:T(256)} fusion(s32[128]{0:T(128)S(1)} %get-tuple-element.6, s32[136]{0:T(256)S(1)} %get-tuple-element.7, s32[128]{0:T(128)S(1)} %select_reduce_fusion.1, s32[136]{0:T(256)S(1)} %get-tuple-element.8, s32[128]{0:T(128)S(1)} %get-tuple-element.5), kind=kLoop, calls=%fused_computation | loop fusion | flops 156536 | bytes 3168 | tf_op jit(solution)/shard_map/reduce_sum | solution.py:444
  1.6 49.2 %layer.1 = bf16[16,4,768]{2,1,0:T(4,128)(2,1)} custom-call(s32[136]{0:T(256)} %select_reduce_fusion.places, s32[128]{0:T(128)} %lengths.1, s32[128]{0:T(128)} %page_request.1, s32[128]{0:T(128)} %page_block.1, bf16[16,4,3072]{2,1,0:T(4,128)(2,1)} %tok.1, bf16[3072]{0:T(1024)(128)(2,1)} %gain1.1, bf16[3072]{0:T(1024)(128)(2,1)} %gain2.1, ...), custom_call_target="tpu_custom_call" | custom-call | flops 6174015488 | bytes 48234496 | tf_op jit(solution)/shard_map/layer/pallas_call | solution.py:468
  50.8 1.6 %copy.18 = bf16[16,4,768]{2,1,0:T(4,128)(2,1)} copy(bf16[16,4,768]{2,1,0:T(4,128)(2,1)} %layer.1) | data formatting | bytes 196608
  (1 shorter events, 0.0 us)

commit v3 on v2

--- a/solution.py
+++ b/solution.py
@@ -18,6 +18,7 @@
 ROWS = 16
 UNROLL = 12
 SHORT_UNROLL = 4
+SHORT_FIRST = 1
 MESH = pl.DeviceIdType.MESH
 F32 = jnp.float32
 BF16 = jnp.bfloat16
@@ -37,7 +38,7 @@
     out,
     wq_v, wk_v, wv_v, wo_v, wg_v, wu_v, wd_v, kc_v, vc_v,
     xf, cos, sin, nrm, qkv, qf, kf, vf, qs, ks, vs, so, sm, sl, ql, oo, om, ol, mj, pj, parts,
-    att, s1, r1, own, s2, r2, res, act, s4, r4, s5, r5,
+    att, s1, r1, own, s2, r2, res, scales, gates, ups, act, s4, r4, s5, r5,
     w_sem, qsend, qrecv, psend, precv,
     s1_sem, r1_sem, s2_sem, r2_sem, s3_sem, r3_sem, s4_sem, r4_sem, s5_sem, r5_sem,
 ):
@@ -67,8 +68,6 @@
     for d in range(1, xs):
         pl.semaphore_signal(barrier, inc=1, device_id=(s, lax.rem(x + d, xs) * 2 + c), device_id_type=MESH)
 
-    loads[3].start()
-
     for r in range(req_dev):
         xf[fresh * r : fresh * r + fresh, :] = tok[r].astype(F32)
     for i in range(rows // 16):
@@ -92,6 +91,7 @@
 
     heads = kv * group
     loads[0].wait()
+    loads[3].start()
     loads[4].start()
     for lo in range(0, heads * head, 256):
         hi = min(lo + 256, heads * head)
@@ -182,9 +182,9 @@
                 so[h, span, :] += o[h * ROWS : (h + 1) * ROWS, h * head : (h + 1) * head]
         return carry
 
-    lax.fori_loop(0, req_dev // SHORT_UNROLL, short_step, 0)
     loads[7].start()
     loads[8].start()
+    lax.fori_loop(0, SHORT_FIRST, short_step, 0)
 
     for j in range(n_long):
         @pl.when(s != j * step)
@@ -271,6 +271,8 @@
         def _():
             part_copy(j).start()
 
+    lax.fori_loop(SHORT_FIRST, req_dev // SHORT_UNROLL, short_step, 0)
+
     @pl.when(is_home)
     def _():
         for d in range(1, seqs):
@@ -322,13 +324,11 @@
     loads[5].wait()
     started = []
     first_sum = [to_mate(s1.at[k], r1.at[k], s1_sem.at[k], r1_sem.at[k]) for k in range(xs)]
+    crossing = {}
     for k in range(xs):
         s1[k] = mm(att[...], block(wo_v, (1 - c) * xs + k)).astype(BF16)
         first_sum[k].start()
-    for k in range(xs):
         own[k] = mm(att[...], block(wo_v, c * xs + k))
-    crossing = {}
-    for k in range(xs):
         first_sum[k].wait_recv()
         total = own[k] + r1[k].astype(F32)
         own[k] = total
@@ -336,6 +336,27 @@
         for d in range(1, xs):
             crossing[k, d] = across(s2.at[k], r2.at[d - 1, k], s2_sem.at[d - 1, k], r2_sem.at[d - 1, k], d)
             crossing[k, d].start()
+    loads[6].wait()
+    loads[7].wait()
+    scales[...] = gain2[...].astype(F32).reshape(1, width)
+
+    def feed(b, square):
+        v = res[b].astype(F32)
+        entering = (v * block(scales, b)).astype(BF16)
+        span = pl.ds(pl.multiple_of(b * bw, 128), bw)
+        for lo in range(0, act.shape[1], 256):
+            gate = mm(entering, wg_v[span, lo : lo + 256])
+            up = mm(entering, wu_v[span, lo : lo + 256])
+            if square is None:
+                gates[:, lo : lo + 256] = gate
+                ups[:, lo : lo + 256] = up
+            else:
+                gates[:, lo : lo + 256] += gate
+                ups[:, lo : lo + 256] += up
+        more = jnp.sum(v * v, axis=-1, keepdims=True)
+        return more if square is None else square + more
+
+    square = None
     spread = []
     for k in range(xs):
         b = c * xs + k
@@ -347,38 +368,25 @@
         copy = to_mate(res.at[b], res.at[b], s3_sem.at[k], r3_sem.at[k])
         copy.start()
         spread.append(copy)
+        square = feed(b, square)
     for k in range(xs):
         b = (1 - c) * xs + k
         to_mate(res.at[b], res.at[b], s3_sem.at[k], r3_sem.at[k]).wait_recv()
-
-    square = jnp.zeros((rows, 1), F32)
-    for b in range(tens):
-        v = res[b].astype(F32)
-        square = square + jnp.sum(v * v, axis=-1, keepdims=True)
+        square = feed(b, square)
     inverse = lax.rsqrt(square / width + EPSILON)
-    scales = gain2[...].astype(F32).reshape(1, width)
-    for b in range(tens):
-        cols = slice(b * bw, (b + 1) * bw)
-        nrm[:, cols] = (res[b].astype(F32) * inverse * scales[:, cols]).astype(BF16)
-
-    loads[6].wait()
-    loads[7].wait()
     for lo in range(0, act.shape[1], 256):
-        gate = mm(nrm[...], wg_v[:, lo : lo + 256])
-        up = mm(nrm[...], wu_v[:, lo : lo + 256])
+        gate = gates[:, lo : lo + 256] * inverse
+        up = ups[:, lo : lo + 256] * inverse
         act[:, lo : lo + 256] = (gate / (1.0 + jnp.exp(-gate)) * up).astype(BF16)
 
     loads[8].wait()
-    pair_sum = []
+    pair_sum, last = [], []
     for k in range(xs):
         to = lax.rem(x + 1 + k, xs)
         s4[k] = mm(act[...], block(wd_v, to * 2 + 1 - c)).astype(BF16)
         copy = to_mate(s4.at[k], r4.at[k], s4_sem.at[k], r4_sem.at[k])
         copy.start()
         pair_sum.append(copy)
-    last = []
-    for k in range(xs):
-        to = lax.rem(x + 1 + k, xs)
         total = mm(act[...], block(wd_v, to * 2 + c))
         pair_sum[k].wait_recv()
         total = total + r4[k].astype(F32)
@@ -459,7 +467,7 @@
         vm((rows, kv * group * head), BF16),
         vm((xs, rows, bw), BF16), vm((xs, rows, bw), BF16), vm((xs, rows, bw)),
         vm((xs, rows, bw), BF16), vm((xs - 1, xs, rows, bw), BF16), vm((tens, rows, bw), BF16),
-        vm((rows, hidden), BF16),
+        vm((1, width)), vm((rows, hidden)), vm((rows, hidden)), vm((rows, hidden), BF16),
         vm((xs, rows, bw), BF16), vm((xs, rows, bw), BF16), vm((xs - 1, rows, bw), BF16), vm((xs - 1, rows, bw), BF16),
         dma(9), dma(seqs - 1), dma(n_long), dma(n_long), dma(seqs),
         dma(xs), dma(xs), dma(xs - 1, xs), dma(xs - 1, xs), dma(xs), dma(xs), dma(xs), dma(xs), dma(xs - 1), dma(xs - 1),

time: 52.5 us -> 46.3 us (0.88)
  Pallas kernels: 49.2 us -> 43 us
    pallas_call x1, Pallas kernels: 49.2 us -> 43 us  [per_device(): pl.pallas_call(functools.partial(layer_kernel, seqs, tens, n_long, others...]
where the time goes in v3:
time: 46.3 us; the launch traced here: 46.1 us
  Pallas kernels  43 us (93%)
  other arithmetic  1.58 us (3%)
  local copies, waits for them, and re-layouts  1.57 us (3%)
    pallas_call x1, Pallas kernels, per_device(): pl.pallas_call(functools.partial(layer_kernel, seqs, tens, n_long, others...  43 us
    unnamed x1, local copies, waits for them, and re-layouts  1.57 us

profile of v3, /device:TPU:0, one launch (start us, length us, event | category | flops | bytes accessed | tf_op | source)
XLA Modules:
  0.0 46.1 jit_solution(11471151364373056957)
XLA Ops:
  0.0 0.7 %and_select_fusion = (s32[128]{0:T(128)S(1)}, s32[128]{0:T(128)S(1)}) fusion(s32[128]{0:T(128)} %page_block.1, s32[128]{0:T(128)} %page_request.1, s32[]{:T(128)S(6)} %mul.6), kind=kLoop, calls=%fused_computation.8 | loop fusion | flops 2560 | bytes 2052 | tf_op jit(solution)/shard_map/jit(_where)/select_n | solution.py:443
  0.7 0.1 select_reduce_fusion.1
  0.8 0.8 %select_reduce_fusion.places = s32[136]{0:T(256)} fusion(s32[128]{0:T(128)S(1)} %get-tuple-element.6, s32[136]{0:T(256)S(1)} %get-tuple-element.7, s32[128]{0:T(128)S(1)} %select_reduce_fusion.1, s32[136]{0:T(256)S(1)} %get-tuple-element.8, s32[128]{0:T(128)S(1)} %get-tuple-element.5), kind=kLoop, calls=%fused_computation | loop fusion | flops 156536 | bytes 3168 | tf_op jit(solution)/shard_map/reduce_sum | solution.py:452
  1.6 43.0 %layer.1 = bf16[16,4,768]{2,1,0:T(4,128)(2,1)} custom-call(s32[136]{0:T(256)} %select_reduce_fusion.places, s32[128]{0:T(128)} %lengths.1, s32[128]{0:T(128)} %page_request.1, s32[128]{0:T(128)} %page_block.1, bf16[16,4,3072]{2,1,0:T(4,128)(2,1)} %tok.1, bf16[3072]{0:T(1024)(128)(2,1)} %gain1.1, bf16[3072]{0:T(1024)(128)(2,1)} %gain2.1, ...), custom_call_target="tpu_custom_call" | custom-call | flops 6174015488 | bytes 48234496 | tf_op jit(solution)/shard_map/layer/pallas_call | solution.py:476
  44.6 1.6 %copy.18 = bf16[16,4,768]{2,1,0:T(4,128)(2,1)} copy(bf16[16,4,768]{2,1,0:T(4,128)(2,1)} %layer.1) | data formatting | bytes 196608
  (1 shorter events, 0.0 us)

commit v4 on v3

--- a/solution.py
+++ b/solution.py
@@ -16,8 +16,9 @@
 STRIDE = 32
 SHORT_BLK = 4
 ROWS = 16
-UNROLL = 12
-SHORT_UNROLL = 4
+UNROLL = 24
+MERGE_UNROLL = 12
+SHORT_UNROLL = 8
 SHORT_FIRST = 1
 MESH = pl.DeviceIdType.MESH
 F32 = jnp.float32
@@ -227,22 +228,22 @@
     lax.fori_loop(0, others // UNROLL, long_step, 0)
 
     def top_step(i, carry):
-        for u in range(4):
-            p = i * 4 + u
+        for u in range(MERGE_UNROLL):
+            p = i * MERGE_UNROLL + u
             m = om[p]
             owner = entry(first + p)[2]
             carry = tuple(jnp.maximum(carry[j], m + jnp.where(owner == j, 0.0, NEGATIVE)) for j in range(n_long))
         return carry
 
     floor = jnp.full((kv, ROWS, head), FLOOR, F32)
-    tops = lax.fori_loop(0, others // 4, top_step, (floor,) * n_long)
+    tops = lax.fori_loop(0, others // MERGE_UNROLL, top_step, (floor,) * n_long)
     for j in range(n_long):
         mj[j] = tops[j]
 
     def sum_step(i, carry):
         sums, totals = carry
-        for u in range(4):
-            p = i * 4 + u
+        for u in range(MERGE_UNROLL):
+            p = i * MERGE_UNROLL + u
             owner = entry(first + p)[2]
             e = jnp.exp(om[p] - mj[owner])
             o = e * oo[p]
@@ -253,12 +254,17 @@
         return sums, totals
 
     zero = jnp.zeros((kv, ROWS, head), F32)
-    sums, totals = lax.fori_loop(0, others // 4, sum_step, ((zero,) * n_long, (zero,) * n_long))
-    low = lane_mask((ROWS, head), 1) < head // 2
+    sums, totals = lax.fori_loop(0, others // MERGE_UNROLL, sum_step, ((zero,) * n_long, (zero,) * n_long))
+    lanes = head // (2 * kv)
+    part_of = lane_mask((ROWS, head), 1) // lanes
     for j in range(n_long):
         for h in range(kv):
-            pj[j, h, 0] = sums[j][h]
-            pj[j, h, 1] = jnp.where(low, tops[j][h], totals[j][h])
+            pj[j, h] = sums[j][h]
+        packed = tops[j][0]
+        for h in range(kv):
+            packed = jnp.where(part_of == 2 * h, tops[j][h], packed)
+            packed = jnp.where(part_of == 2 * h + 1, totals[j][h], packed)
+        pj[j, kv] = packed
 
     def part_copy(j):
         return pltpu.make_async_remote_copy(
@@ -283,12 +289,12 @@
             ).wait_recv()
         for h in range(kv):
             pieces = [(sm[h, :ROWS, :1], sl[h, :ROWS, :1], so[h, :ROWS, :])]
-            blocks = [(pj[home, h, 0], pj[home, h, 1])]
+            blocks = [(pj[home, h], pj[home, kv])]
             for d in range(1, seqs):
                 src = lax.rem(s + d, seqs)
-                blocks.append((parts[src, h, 0], parts[src, h, 1]))
+                blocks.append((parts[src, h], parts[src, kv]))
             for o, ml in blocks:
-                pieces.append((ml[:, :1], ml[:, head // 2 : head // 2 + 1], o))
+                pieces.append((ml[:, 2 * h * lanes : 2 * h * lanes + 1], ml[:, (2 * h + 1) * lanes : (2 * h + 1) * lanes + 1], o))
             m = functools.reduce(jnp.maximum, [piece[0] for piece in pieces])
             l = jnp.zeros((ROWS, 1), F32)
             o = jnp.zeros((ROWS, head), F32)
@@ -463,7 +469,7 @@
         vm(tall, BF16), vm(tall, BF16), vm(tall, BF16), vm(tall), vm(tall), vm(tall),
         vm((n_long, kv, ROWS, head), BF16),
         vm((others, kv, ROWS, head)), vm((others, kv, ROWS, head)), vm((others, kv, ROWS, head)),
-        vm((n_long, kv, ROWS, head)), vm((n_long, kv, 2, ROWS, head)), vm((seqs, kv, 2, ROWS, head)),
+        vm((n_long, kv, ROWS, head)), vm((n_long, kv + 1, ROWS, head)), vm((seqs, kv + 1, ROWS, head)),
         vm((rows, kv * group * head), BF16),
         vm((xs, rows, bw), BF16), vm((xs, rows, bw), BF16), vm((xs, rows, bw)),
         vm((xs, rows, bw), BF16), vm((xs - 1, xs, rows, bw), BF16), vm((tens, rows, bw), BF16),

time: 46.3 us -> 46.1 us (level)
  no operation moved by 1% of the time
where the time goes in v4:
time: 46.1 us; the launch traced here: 46 us
  Pallas kernels  42.8 us (93%)
  other arithmetic  1.58 us (3%)
  local copies, waits for them, and re-layouts  1.57 us (3%)
    pallas_call x1, Pallas kernels, per_device(): pl.pallas_call(functools.partial(layer_kernel, seqs, tens, n_long, others...  42.8 us
    unnamed x1, local copies, waits for them, and re-layouts  1.57 us

profile of v4, /device:TPU:0, one launch (start us, length us, event | category | flops | bytes accessed | tf_op | source)
XLA Modules:
  0.0 46.0 jit_solution(18316374826581082452)
XLA Ops:
  0.0 0.7 %and_select_fusion = (s32[128]{0:T(128)S(1)}, s32[128]{0:T(128)S(1)}) fusion(s32[128]{0:T(128)} %page_block.1, s32[128]{0:T(128)} %page_request.1, s32[]{:T(128)S(6)} %mul.6), kind=kLoop, calls=%fused_computation.8 | loop fusion | flops 2560 | bytes 2052 | tf_op jit(solution)/shard_map/jit(_where)/select_n | solution.py:449
  0.7 0.1 select_reduce_fusion.1
  0.8 0.8 %select_reduce_fusion.places = s32[136]{0:T(256)} fusion(s32[128]{0:T(128)S(1)} %get-tuple-element.6, s32[136]{0:T(256)S(1)} %get-tuple-element.7, s32[128]{0:T(128)S(1)} %select_reduce_fusion.1, s32[136]{0:T(256)S(1)} %get-tuple-element.8, s32[128]{0:T(128)S(1)} %get-tuple-element.5), kind=kLoop, calls=%fused_computation | loop fusion | flops 156536 | bytes 3168 | tf_op jit(solution)/shard_map/reduce_sum | solution.py:458
  1.6 42.8 %layer.1 = bf16[16,4,768]{2,1,0:T(4,128)(2,1)} custom-call(s32[136]{0:T(256)} %select_reduce_fusion.places, s32[128]{0:T(128)} %lengths.1, s32[128]{0:T(128)} %page_request.1, s32[128]{0:T(128)} %page_block.1, bf16[16,4,3072]{2,1,0:T(4,128)(2,1)} %tok.1, bf16[3072]{0:T(1024)(128)(2,1)} %gain1.1, bf16[3072]{0:T(1024)(128)(2,1)} %gain2.1, ...), custom_call_target="tpu_custom_call" | custom-call | flops 6174015488 | bytes 48234496 | tf_op jit(solution)/shard_map/layer/pallas_call | solution.py:482
  44.4 1.6 %copy.18 = bf16[16,4,768]{2,1,0:T(4,128)(2,1)} copy(bf16[16,4,768]{2,1,0:T(4,128)(2,1)} %layer.1) | data formatting | bytes 196608
  (1 shorter events, 0.0 us)
